TPU v7x, 32 devices: a whole 2x2x4 slice. The times are simulated.
32 devices in a mesh: row: 4 (over y, x), col: 4 (over z), depth: 2 (over core).
Axes of the slice: x: 2, y: 2, z: 4, core: 2. Of those that a mesh axis runs over, the one named last changes fastest.
Arguments:
- tokens: bfloat16 [512, 12288], P(('col', 'depth'), 'row'), may hold values from -6 to 6
- weight: bfloat16 [12288, 24576], P('row', ('col', 'depth')), may hold values from -0.0546875 to 0.0546875
- cotangent: bfloat16 [512, 24576], P('row', ('col', 'depth')), may hold values from -6 to 6
Outputs:
- hidden: bfloat16 [512, 24576], P('row', ('col', 'depth'))
- input_grad: bfloat16 [512, 12288], P(('col', 'depth'), 'row')
- weight_grad: float32 [12288, 24576], P('row', ('col', 'depth'))
All inputs are finite; a program needn't handle non-finite values.
Results may differ from a plain program's by a relative error of at most 0.02.
Values may be sent and summed in bfloat16 or wider, within the bound.
A program may use at most 192 MiB of HBM per device.

v0:
```python
import jax
import jax.numpy as jnp
from jax import lax
from jax.sharding import PartitionSpec as P

root_coef = 0.7978845608
cubic_coef = 0.044715


def gelu_parts(preact):
    inner = root_coef * (preact + cubic_coef * preact * preact * preact)
    tanh_val = jnp.tanh(inner)
    value = 0.5 * preact * (1.0 + tanh_val)
    slope = 0.5 * (1.0 + tanh_val) + 0.5 * preact * (1.0 - tanh_val * tanh_val) * root_coef * (
        1.0 + 3.0 * cubic_coef * preact * preact
    )
    return (value, slope)


def shards(tokens, weight, cotangent):
    whole_tokens = lax.all_gather(tokens, ("col", "depth"), axis=0, tiled=True)
    partial_value = jnp.dot(whole_tokens, weight, preferred_element_type=jnp.float32)
    own_rows = lax.psum_scatter(
        partial_value.astype(jnp.bfloat16), "row", scatter_dimension=0, tiled=True
    ).astype(jnp.float32)
    value_own, slope_own = gelu_parts(own_rows)
    hidden = value_own.astype(jnp.bfloat16)
    grad_own = (cotangent.astype(jnp.float32) * slope_own).astype(jnp.bfloat16)
    grad_all = lax.all_gather(grad_own, "row", axis=0, tiled=True)
    token_count = whole_tokens.shape[0]
    weight_grad = lax.dot_general(
        whole_tokens, grad_all, (((0,), (0,)), ((), ())), preferred_element_type=jnp.float32
    ) * token_count ** (-0.5)
    summed_grad = lax.psum_scatter(
        lax.dot_general(
            grad_all, weight, (((1,), (1,)), ((), ())), preferred_element_type=jnp.float32
        ).astype(jnp.bfloat16),
        ("col", "depth"),
        scatter_dimension=0,
        tiled=True,
    )
    return (hidden, summed_grad, weight_grad)


def solution(mesh):
    in_specs = (P(("col", "depth"), "row"), P("row", ("col", "depth")), P("row", ("col", "depth")))
    out_specs = (P("row", ("col", "depth")), P(("col", "depth"), "row"), P("row", ("col", "depth")))
    return jax.shard_map(shards, mesh=mesh, in_specs=in_specs, out_specs=out_specs, check_vma=False)
```

profile of v0, /device:TPU:0, one launch (start us, length us, event | category | flops | bytes accessed | tf_op | source)
XLA Modules:
  0.0 236.2 jit_solution(8989319296869341704)
XLA Ops:
  7.2 0.0 all-gather.3.cloned.1.call-start
  7.2 0.7 all-gather.3.cloned.1.call-update
  7.9 0.0 reduce-scatter.3.cloned.1.call-start
  7.9 42.7 %all-gather.3.cloned.1.call-done = bf16[512,3072]{1,0:T(8,128)(2,1)} async-done(((bf16[64,3072]{1,0:T(8,128)(2,1)}), bf16[512,3072]{1,0:T(8,128)(2,1)}) %all-gather.3.cloned.1.call-update) | async-done | bytes 3145744 | tf_op jit(solution)/shard_map/all_gather | solution.py:21
  50.7 15.8 %convolution_convert_fusion.1 = bf16[512,3072]{1,0:T(8,128)(2,1)} fusion(bf16[512,3072]{1,0:T(8,128)(2,1)} %all-gather.3.cloned.1.call-done, bf16[3072,3072]{1,0:T(8,128)(2,1)} %param.4), kind=kOutput, calls=%fused_computation.2 | convolution fusion | flops 9665249280 | bytes 25165824 | tf_op jit(solution)/shard_map/dot_general | solution.py:22
  66.4 0.0 copy-start
  66.4 0.0 reduce-scatter.3.cloned.1.call-update
  66.5 0.0 all-gather.5.cloned.1.call-start
  66.5 42.9 %reduce-scatter.3.cloned.1.call-done = bf16[128,3072]{1,0:T(8,128)(2,1)} async-done(((bf16[512,3072]{1,0:T(8,128)(2,1)}), bf16[128,3072]{1,0:T(8,128)(2,1)}) %reduce-scatter.3.cloned.1.call-update) | async-done | bytes 786448 | tf_op jit(solution)/shard_map/reduce_scatter | solution.py:23
  109.4 0.0 copy-done
  109.4 3.4 %fusion.7 = (bf16[128,3072]{1,0:T(8,128)(2,1)}, bf16[128,3072]{1,0:T(8,128)(2,1)}) fusion(bf16[128,3072]{1,0:T(8,128)(2,1)} %reduce-scatter.3.cloned.1.call-done, bf16[128,3072]{1,0:T(8,128)(2,1)S(1)} %copy-done), kind=kLoop, calls=%fused_computation.17 | loop fusion | flops 9043968 | bytes 3145728 | tf_op jit(solution)/shard_map/convert_element_type | solution.py:28
  112.9 0.0 all-gather.5.cloned.1.call-update
  112.9 0.2 reduce-scatter.5.cloned.1.call-start
  113.1 43.9 %all-gather.5.cloned.1.call-done = bf16[512,3072]{1,0:T(8,128)(2,1)} async-done(((bf16[128,3072]{1,0:T(8,128)(2,1)}), bf16[512,3072]{1,0:T(8,128)(2,1)}) %all-gather.5.cloned.1.call-update) | async-done | bytes 3145744 | tf_op jit(solution)/shard_map/all_gather | solution.py:29
  157.0 15.9 %convolution_convert_fusion = bf16[512,3072]{1,0:T(8,128)(2,1)} fusion(bf16[512,3072]{1,0:T(8,128)(2,1)} %all-gather.5.cloned.1.call-done, bf16[3072,3072]{1,0:T(8,128)(2,1)} %param.4), kind=kOutput, calls=%fused_computation.1 | convolution fusion | flops 9665249280 | bytes 25165824 | tf_op jit(solution)/shard_map/dot_general | solution.py:35
  172.9 0.0 copy-start.1
  172.9 0.0 reduce-scatter.5.cloned.1.call-update
  173.0 1.9 copy-done.1
  174.8 18.0 %multiply_bitcast_fusion = f32[3072,3072]{0,1:T(8,128)} fusion(bf16[512,3072]{1,0:T(8,128)(2,1)} %all-gather.5.cloned.1.call-done, bf16[512,3072]{1,0:T(8,128)(2,1)S(1)} %copy-done.1), kind=kOutput, calls=%fused_computation | convolution fusion | flops 9673113600 | bytes 44040192 | tf_op jit(solution)/shard_map/dot_general | solution.py:31
  192.8 36.9 %copy.6 = f32[3072,3072]{1,0:T(8,128)} copy(f32[3072,3072]{0,1:T(8,128)} %multiply_bitcast_fusion) | data formatting | bytes 75497472
  229.7 0.0 reduce-scatter.5.cloned.1.call-done
Async XLA Ops:
  7.2 43.5 %all-gather.3.cloned.1.call-start = ((), (), s32[]{:S(2)}) async-start(), calls=%async_computation.2 | async-start | bytes 3538944 | tf_op jit(solution)/shard_map/all_gather | solution.py:21
  7.9 101.5 %reduce-scatter.3.cloned.1.call-start = ((), (), s32[]{:S(2)}) async-start(), calls=%async_computation.3 | async-start | bytes 3932160 | tf_op jit(solution)/shard_map/reduce_scatter | solution.py:23
  66.4 43.0 %copy-start = (bf16[128,3072]{1,0:T(8,128)(2,1)S(1)}, bf16[128,3072]{1,0:T(8,128)(2,1)}, u32[]{:S(2)}) copy-start(bf16[128,3072]{1,0:T(8,128)(2,1)} %param.5) | copy-start | bytes 2359300
  66.5 90.6 %all-gather.5.cloned.1.call-start = ((), (), s32[]{:S(2)}) async-start(), calls=%async_computation.4 | async-start | bytes 3932160 | tf_op jit(solution)/shard_map/all_gather | solution.py:29
  112.9 116.8 %reduce-scatter.5.cloned.1.call-start = ((), (), s32[]{:S(2)}) async-start(), calls=%async_computation.5 | async-start | bytes 3538944 | tf_op jit(solution)/shard_map/reduce_scatter | solution.py:34
  172.9 1.9 copy-start.1
Sparse Core Ops, SparseCore 0:
  9.6 40.9 all-gather.2
  66.6 42.8 reduce-scatter.2
  113.0 43.9 all-gather.4
  173.1 40.3 reduce-scatter.4
where the time goes:
time: 237 us; the launch traced here: 236 us
  waiting for transfers between devices  130 us (55%)
  matrix products  49.7 us (21%)
  local copies, waits for them, and re-layouts  38.7 us (16%)
  between operations  13.8 us (6%)
  other arithmetic  3.44 us (1%)
    all_gather x1, waiting for transfers between devices, shards(): grad_all = lax.all_gather(grad_own, 'row', axis=0, tiled=True)  43.9 us
    reduce_scatter x1, waiting for transfers between devices, shards(): lax.psum_scatter(partial_value.astype(jnp.bfloat16), 'row', scatter_dimen...  42.9 us
    all_gather x1, waiting for transfers between devices, shards(): whole_tokens = lax.all_gather(tokens, ('col', 'depth'), axis=0, tiled=True)  42.7 us
    unnamed x5, local copies, waits for them, and re-layouts  38.7 us
    dot_general x1, matrix products, shards(): lax.dot_general(whole_tokens, grad_all, (((0,), (0,)), ((), ())), preferr...  18 us
    dot_general x1, matrix products, shards(): lax.dot_general(grad_all, weight, (((1,), (1,)), ((), ())), preferred_ele...  15.9 us
    dot_general x1, matrix products, shards(): jnp.dot(whole_tokens, weight, preferred_element_type=jnp.float32)  15.8 us
  transfers between devices with their start and end apart: 4, of which 3 were waited for; matrix products, arithmetic and copies ran while one was open for 23% of the time, Pallas kernels for 0%

commit v1 on v0

v1 whole, which is shorter than its diff:
```python
import functools

import jax
import jax.numpy as jnp
from jax import lax
from jax.experimental import pallas as pl
from jax.experimental.pallas import tpu as pltpu
from jax.sharding import PartitionSpec as P

MESH = pl.DeviceIdType.MESH
root_coef = 0.7978845608
cubic_coef = 0.044715
chunks = 2


def gelu_parts(preact):
    inner = root_coef * (preact + cubic_coef * preact * preact * preact)
    tanh_val = jnp.tanh(inner)
    value = 0.5 * preact * (1.0 + tanh_val)
    slope = 0.5 * (1.0 + tanh_val) + 0.5 * preact * (1.0 - tanh_val * tanh_val) * root_coef * (
        1.0 + 3.0 * cubic_coef * preact * preact
    )
    return (value, slope)


def tile_of(extent, most):
    return max(t for t in range(128, min(most, extent) + 1, 128) if extent % t == 0)


def chain_kernel(
    n_row, n_col, n_depth, f_tile, d_tile,
    tok_ref, w_hbm, cot_ref,
    hid_ref, ing_ref, x_ref, g_ref,
    w_ref, part_ref, relay_a, relay_b, sum_a, sum_b, from_x, from_y,
    back_ref, sib_ref, chip_ref, line_ref,
    w_sem, own_sem,
    line_send, sib_send, x_recv,
    rs_send, rs_recv, ag_send, ag_recv,
    sb_send, sb_recv, zl_send, zl_recv,
):
    f32, bf16 = jnp.float32, jnp.bfloat16
    row, col, depth = lax.axis_index("row"), lax.axis_index("col"), lax.axis_index("depth")
    blocks = n_col * n_depth
    own_tokens, d_size = tok_ref.shape
    f_size = cot_ref.shape[1]
    piece = own_tokens // chunks
    chunk_rows = blocks * piece
    row_rows = chunk_rows // n_row
    half = row_rows // 2
    per_row = blocks // n_row
    nf, nd = f_size // f_tile, d_size // d_tile

    row_x = row + 1 - 2 * lax.rem(row, 2)
    row_y = lax.rem(row + 2, 4)
    row_z = lax.rem(row_x + 2, 4)
    dev_x = (row_x, col, depth)
    dev_y = (row_y, col, depth)
    cols = [lax.rem(col + o, n_col) for o in range(n_col)]
    depths = [lax.rem(depth + o, n_depth) for o in range(n_depth)]
    dev_c = [(row, c, depth) for c in cols]
    dev_d = [(row, col, d) for d in depths]

    sends = []

    def push(src, dst, send_sem, recv_sem, device):
        copy = pltpu.make_async_remote_copy(
            src_ref=src, dst_ref=dst, send_sem=send_sem, recv_sem=recv_sem,
            device_id=device, device_id_type=MESH,
        )
        copy.start()
        sends.append(copy)

    def arrived(dst, recv_sem):
        pltpu.make_async_remote_copy(
            src_ref=dst, dst_ref=dst, send_sem=recv_sem, recv_sem=recv_sem,
            device_id=dev_x, device_id_type=MESH,
        ).wait_recv()

    def al(v, m):
        return pl.multiple_of(v, m)

    def x_at(k, block):
        return x_ref.at[pl.ds(al(k * chunk_rows + block * piece, piece), piece), :]

    def rows_at(ref, k, r, j, part=None):
        start = k * chunk_rows + r * row_rows
        size = row_rows
        if part is not None:
            start, size = start + part * half, half
        return ref.at[pl.ds(al(start, half), size), pl.ds(j * f_tile, f_tile)]

    def half_at(ref, k, j):
        return ref.at[pl.ds(k * half, half), pl.ds(j * f_tile, f_tile)]

    def sum_at(ref, k, j, part):
        return ref.at[pl.ds(k * row_rows + part * half, half), pl.ds(j * f_tile, f_tile)]

    weight_copy = pltpu.make_async_copy(w_hbm, w_ref, w_sem)
    weight_copy.start()

    barrier = pltpu.get_barrier_semaphore()
    greet = dev_c[1:] + dev_d[1:] + [dev_x, dev_y]
    for device in greet:
        pl.semaphore_signal(barrier, inc=1, device_id=device, device_id_type=MESH)
    pl.semaphore_wait(barrier, len(greet))

    me = col * n_depth + depth
    own_copies = []
    for k in range(chunks):
        src = tok_ref.at[pl.ds(k * piece, piece), :]
        for o in range(1, n_col):
            push(src, x_at(k, me), line_send.at[k, o], x_recv.at[k, me], dev_c[o])
        for o in range(1, n_depth):
            push(src, x_at(k, me), sib_send.at[k, o, 0], x_recv.at[k, me], dev_d[o])
        own = pltpu.make_async_copy(src, x_at(k, me), own_sem.at[k])
        own.start()
        own_copies.append(own)

    def gather_tokens(k):
        for o in range(1, n_col):
            block = cols[o] * n_depth + depth
            arrived(x_at(k, block), x_recv.at[k, block])
            for q in range(1, n_depth):
                push(x_at(k, block), x_at(k, block), sib_send.at[k, q, o], x_recv.at[k, block], dev_d[q])
        for q in range(1, n_depth):
            for o in range(n_col):
                block = cols[o] * n_depth + depths[q]
                arrived(x_at(k, block), x_recv.at[k, block])
        own_copies[k].wait()

    def up(k, j):
        value = jnp.dot(
            x_ref[pl.ds(k * chunk_rows, chunk_rows), :], w_ref[:, pl.ds(j * f_tile, f_tile)],
            preferred_element_type=f32,
        )
        part_ref[pl.ds(k * chunk_rows, chunk_rows), pl.ds(j * f_tile, f_tile)] = value.astype(bf16)
        push(rows_at(part_ref, k, row_z, j, 0), half_at(relay_a, k, j), rs_send.at[k, j, 0], rs_recv.at[k, j, 0], dev_x)
        push(rows_at(part_ref, k, row_z, j, 1), half_at(relay_b, k, j), rs_send.at[k, j, 1], rs_recv.at[k, j, 1], dev_y)
        push(rows_at(part_ref, k, row_x, j, 0), sum_at(from_x, k, j, 0), rs_send.at[k, j, 2], rs_recv.at[k, j, 2], dev_x)
        push(rows_at(part_ref, k, row_y, j, 1), sum_at(from_y, k, j, 1), rs_send.at[k, j, 3], rs_recv.at[k, j, 3], dev_y)

    def relay(k, j):
        arrived(half_at(relay_a, k, j), rs_recv.at[k, j, 0])
        mine = rows_at(part_ref, k, row_y, j, 0)[...].astype(f32)
        half_at(sum_a, k, j)[...] = (mine + half_at(relay_a, k, j)[...].astype(f32)).astype(bf16)
        push(half_at(sum_a, k, j), sum_at(from_y, k, j, 0), rs_send.at[k, j, 4], rs_recv.at[k, j, 4], dev_y)
        arrived(half_at(relay_b, k, j), rs_recv.at[k, j, 1])
        mine = rows_at(part_ref, k, row_x, j, 1)[...].astype(f32)
        half_at(sum_b, k, j)[...] = (mine + half_at(relay_b, k, j)[...].astype(f32)).astype(bf16)
        push(half_at(sum_b, k, j), sum_at(from_x, k, j, 1), rs_send.at[k, j, 5], rs_recv.at[k, j, 5], dev_x)

    def activate(k, j):
        arrived(sum_at(from_x, k, j, 0), rs_recv.at[k, j, 2])
        arrived(sum_at(from_y, k, j, 1), rs_recv.at[k, j, 3])
        arrived(sum_at(from_y, k, j, 0), rs_recv.at[k, j, 4])
        arrived(sum_at(from_x, k, j, 1), rs_recv.at[k, j, 5])
        span = pl.ds(j * f_tile, f_tile)
        mine = rows_at(part_ref, k, row, j)[...].astype(f32)
        rows = pl.ds(k * row_rows, row_rows)
        preact = mine + from_x[rows, span].astype(f32) + from_y[rows, span].astype(f32)
        value, slope = gelu_parts(preact)
        value = value.astype(bf16)
        grads = []
        for b in range(per_row):
            local = pl.ds(b * own_tokens + k * piece, piece)
            hid_ref[local, span] = value[b * piece:(b + 1) * piece]
            grads.append((cot_ref[local, span].astype(f32) * slope[b * piece:(b + 1) * piece]).astype(bf16))
        rows_at(g_ref, k, row, j)[...] = jnp.concatenate(grads, axis=0)
        spot = rows_at(g_ref, k, row, j)
        push(spot, spot, ag_send.at[k, j, 0], ag_recv.at[k, j, 0], dev_x)
        push(spot, spot, ag_send.at[k, j, 1], ag_recv.at[k, j, 1], dev_y)

    def forward(k, j):
        arrived(rows_at(g_ref, k, row_x, j), ag_recv.at[k, j, 0])
        spot = rows_at(g_ref, k, row_x, j, 0)
        push(spot, spot, ag_send.at[k, j, 2], ag_recv.at[k, j, 2], dev_y)
        arrived(rows_at(g_ref, k, row_y, j), ag_recv.at[k, j, 1])
        spot = rows_at(g_ref, k, row_y, j, 1)
        push(spot, spot, ag_send.at[k, j, 3], ag_recv.at[k, j, 3], dev_x)

    def gathered(k, j):
        arrived(rows_at(g_ref, k, row_z, j, 0), ag_recv.at[k, j, 2])
        arrived(rows_at(g_ref, k, row_z, j, 1), ag_recv.at[k, j, 3])

    def down(k, i):
        span = pl.ds(i * d_tile, d_tile)
        value = lax.dot_general(
            g_ref[pl.ds(k * chunk_rows, chunk_rows), :], w_ref[span, :],
            (((1,), (1,)), ((), ())), preferred_element_type=f32,
        ).astype(bf16)
        for c in range(n_col):
            for d in range(n_depth):
                start = (c * n_depth + d) * piece
                back_ref[k, d, pl.ds(c * piece, piece), span] = value[start:start + piece]
        for q in range(1, n_depth):
            push(
                back_ref.at[k, depths[q], :, span], sib_ref.at[q - 1, k, :, span],
                sb_send.at[k, i, q], sb_recv.at[k, i, q], dev_d[q],
            )

    def chip_sum(k, i):
        span = pl.ds(i * d_tile, d_tile)
        total = back_ref.at[k, depth][:, span].astype(f32)
        for q in range(1, n_depth):
            arrived(sib_ref.at[q - 1, k, :, span], sb_recv.at[k, i, q])
            total = total + sib_ref[q - 1, k, :, span].astype(f32)
        chip_ref[k, :, span] = total.astype(bf16)
        for o in range(1, n_col):
            push(
                chip_ref.at[k, pl.ds(al(cols[o] * piece, piece), piece), span],
                line_ref.at[o - 1, k, :, span],
                zl_send.at[k, i, o], zl_recv.at[k, i, o], dev_c[o],
            )

    def line_sum(k, i):
        span = pl.ds(i * d_tile, d_tile)
        total = chip_ref.at[k, pl.ds(al(col * piece, piece), piece), span][...].astype(f32)
        for o in range(1, n_col):
            arrived(line_ref.at[o - 1, k, :, span], zl_recv.at[k, i, o])
            total = total + line_ref[o - 1, k, :, span].astype(f32)
        ing_ref[pl.ds(k * piece, piece), span] = total.astype(bf16)

    gather_tokens(0)
    weight_copy.wait()
    for k in range(chunks):
        if k:
            gather_tokens(k)
        for j in range(nf):
            up(k, j)
            if j:
                relay(k, j - 1)
            if k:
                forward(k - 1, j)
        relay(k, nf - 1)
        if k:
            for j in range(nf):
                gathered(k - 1, j)
            for i in range(nd):
                down(k - 1, i)
                if i:
                    chip_sum(k - 1, i - 1)
            chip_sum(k - 1, nd - 1)
        for j in range(nf):
            activate(k, j)
    last = chunks - 1
    for j in range(nf):
        forward(last, j)
    for j in range(nf):
        gathered(last, j)
    for i in range(nd):
        down(last, i)
        if i:
            chip_sum(last, i - 1)
    chip_sum(last, nd - 1)
    for k in range(chunks):
        for i in range(nd):
            line_sum(k, i)
    for copy in sends:
        copy.wait_send()


def chain(n_row, n_col, n_depth, tokens, weight, cotangent):
    own_tokens, d_size = tokens.shape
    own_rows, f_size = cotangent.shape
    bf16 = jnp.bfloat16
    assert n_row == 4 and own_tokens % (16 * chunks) == 0
    blocks = n_col * n_depth
    all_tokens = own_tokens * blocks
    piece = own_tokens // chunks
    f_tile, d_tile = tile_of(f_size, 768), tile_of(d_size, 768)
    nf, nd = f_size // f_tile, d_size // d_tile
    whole = pl.BlockSpec(memory_space=pltpu.VMEM)
    dma = pltpu.SemaphoreType.DMA
    flops = 4 * all_tokens * d_size * f_size
    return pl.pallas_call(
        functools.partial(chain_kernel, n_row, n_col, n_depth, f_tile, d_tile),
        out_shape=[
            jax.ShapeDtypeStruct((own_rows, f_size), bf16),
            jax.ShapeDtypeStruct((own_tokens, d_size), bf16),
            jax.ShapeDtypeStruct((all_tokens, d_size), bf16),
            jax.ShapeDtypeStruct((all_tokens, f_size), bf16),
        ],
        in_specs=[whole, pl.BlockSpec(memory_space=pl.ANY), whole],
        out_specs=[whole] * 4,
        scratch_shapes=[
            pltpu.VMEM((d_size, f_size), bf16),
            pltpu.VMEM((all_tokens, f_size), bf16),
            pltpu.VMEM((own_rows // 2, f_size), bf16),
            pltpu.VMEM((own_rows // 2, f_size), bf16),
            pltpu.VMEM((own_rows // 2, f_size), bf16),
            pltpu.VMEM((own_rows // 2, f_size), bf16),
            pltpu.VMEM((own_rows, f_size), bf16),
            pltpu.VMEM((own_rows, f_size), bf16),
            pltpu.VMEM((chunks, n_depth, n_col * piece, d_size), bf16),
            pltpu.VMEM((n_depth - 1, chunks, n_col * piece, d_size), bf16),
            pltpu.VMEM((chunks, n_col * piece, d_size), bf16),
            pltpu.VMEM((n_col - 1, chunks, piece, d_size), bf16),
            dma, dma((chunks,)),
            dma((chunks, n_col)), dma((chunks, n_depth, n_col)), dma((chunks, blocks)),
            dma((chunks, nf, 6)), dma((chunks, nf, 6)),
            dma((chunks, nf, 4)), dma((chunks, nf, 4)),
            dma((chunks, nd, n_depth)), dma((chunks, nd, n_depth)),
            dma((chunks, nd, n_col)), dma((chunks, nd, n_col)),
        ],
        compiler_params=pltpu.CompilerParams(
            collective_id=0, has_side_effects=True, vmem_limit_bytes=62 * 2**20
        ),
        cost_estimate=pl.CostEstimate(
            flops=flops, bytes_accessed=2 * d_size * f_size, transcendentals=own_rows * f_size
        ),
        name="chain",
    )(tokens, weight, cotangent)


def weight_grad_kernel(scale, f_tile, x_ref, g_ref, out_ref):
    for j in range(g_ref.shape[1] // f_tile):
        span = pl.ds(j * f_tile, f_tile)
        out_ref[:, span] = scale * lax.dot_general(
            x_ref[...], g_ref[:, span], (((0,), (0,)), ((), ())),
            preferred_element_type=jnp.float32,
        )


def weight_grad_of(tokens, grads):
    count, d_size = tokens.shape
    f_size = grads.shape[1]
    d_tile, f_tile = tile_of(d_size, 256), tile_of(f_size, 768)
    return pl.pallas_call(
        functools.partial(weight_grad_kernel, count ** (-0.5), f_tile),
        grid=(d_size // d_tile,),
        out_shape=jax.ShapeDtypeStruct((d_size, f_size), jnp.float32),
        in_specs=[
            pl.BlockSpec((count, d_tile), lambda i: (0, i)),
            pl.BlockSpec((count, f_size), lambda i: (0, 0)),
        ],
        out_specs=pl.BlockSpec((d_tile, f_size), lambda i: (i, 0)),
        compiler_params=pltpu.CompilerParams(vmem_limit_bytes=40 * 2**20),
        cost_estimate=pl.CostEstimate(
            flops=2 * count * d_size * f_size, bytes_accessed=4 * d_size * f_size, transcendentals=0
        ),
        name="weight_grad",
    )(tokens, grads)


def solution(mesh):
    sizes = [mesh.shape[name] for name in ("row", "col", "depth")]

    def shards(tokens, weight, cotangent):
        hidden, input_grad, x_all, g_all = chain(*sizes, tokens, weight, cotangent)
        return (hidden, input_grad, weight_grad_of(x_all, g_all))

    in_specs = (P(("col", "depth"), "row"), P("row", ("col", "depth")), P("row", ("col", "depth")))
    out_specs = (P("row", ("col", "depth")), P(("col", "depth"), "row"), P("row", ("col", "depth")))
    return jax.shard_map(shards, mesh=mesh, in_specs=in_specs, out_specs=out_specs, check_vma=False)
```

time: 237 us -> 147 us (0.62)
  Pallas kernels: 0 us -> 141 us
  waiting for transfers between devices: 130 us -> 0 us
  matrix products: 49.7 us -> 0 us
  local copies, waits for them, and re-layouts: 38.7 us -> 5.4 us
  between operations: 13.8 us -> 0.65 us
  other arithmetic: 3.44 us -> 0 us
    pallas_call x0 -> x2, Pallas kernels: none -> 141 us  [the longest x1 124 us: chain(): pl.pallas_call(functools.partial(chain_kernel, n_row, n_col, n_depth, f_t...]
    all_gather x2 -> x0, waiting for transfers between devices: 86.6 us -> none  [the longest x1 43.9 us: shards(): grad_all = lax.all_gather(grad_own, 'row', axis=0, tiled=True)]
    dot_general x3 -> x0, matrix products: 49.7 us -> none  [the longest x1 18 us: shards(): lax.dot_general(whole_tokens, grad_all, (((0,), (0,)), ((), ())), preferr...]
    reduce_scatter x2 -> x0, waiting for transfers between devices: 42.9 us -> none  [the longest x1 42.9 us: shards(): lax.psum_scatter(partial_value.astype(jnp.bfloat16), 'row', scatter_dimen...]
    unnamed x5 -> x10, local copies, waits for them, and re-layouts: 38.7 us -> 5.4 us
    convert_element_type x1 -> x0, other arithmetic: 3.44 us -> none  [shards(): grad_own = (cotangent.astype(jnp.float32) * slope_own).astype(jnp.bfloat16)]
  transfers between devices with their start and end apart: 4 -> 0, of which waited for: 3 -> 0; matrix products, arithmetic and copies ran while one was open for 23% -> 0% of each run, Pallas kernels for 0% -> 0%
where the time goes in v1:
time: 147 us
  Pallas kernels  141 us (96%)
  local copies, waits for them, and re-layouts  5.4 us (4%)
    pallas_call x1, Pallas kernels, chain(): pl.pallas_call(functools.partial(chain_kernel, n_row, n_col, n_depth, f_t...  124 us
    pallas_call x1, Pallas kernels, weight_grad_of(): pl.pallas_call(functools.partial(weight_grad_kernel, count ** (-0.5), f_t...  17.4 us
    unnamed x10, local copies, waits for them, and re-layouts  5.4 us

profile of v1, /device:TPU:0, one launch (start us, length us, event | category | flops | bytes accessed | tf_op | source)
XLA Modules:
  0.0 146.9 jit_solution(16088571480862610523)
XLA Ops:
  0.6 123.5 %chain.1 = (bf16[128,3072]{1,0:T(8,128)(2,1)}, bf16[64,3072]{1,0:T(8,128)(2,1)}, bf16[512,3072]{1,0:T(8,128)(2,1)}, bf16[512,3072]{1,0:T(8,128)(2,1)}) custom-call(bf16[64,3072]{1,0:T(8,128)(2,1)} %tok_ref.1, bf16[3072,3072]{1,0:T(8,128)(2,1)} %w_hbm.1, bf16[128,3072]{1,0:T(8,128)(2,1)} %cot_ref.1), custom_call_target="tpu_custom_call" | custom-call | flops 19327352832 | bytes 18874368 | tf_op jit(solution)/shard_map/chain/pallas_call | solution.py:275
  124.2 0.0 copy-start
  124.2 1.9 %copy-done = bf16[512,3072]{1,0:T(8,128)(2,1)S(1)} copy-done((bf16[512,3072]{1,0:T(8,128)(2,1)S(1)}, bf16[512,3072]{1,0:T(8,128)(2,1)}, u32[]{:S(2)}) %copy-start) | copy-done | bytes 3145752
  126.1 0.0 copy-start.1
  126.1 1.9 %copy-done.1 = bf16[512,3072]{1,0:T(8,128)(2,1)S(1)} copy-done((bf16[512,3072]{1,0:T(8,128)(2,1)S(1)}, bf16[512,3072]{1,0:T(8,128)(2,1)}, u32[]{:S(2)}) %copy-start.1) | copy-done | bytes 3145752
  128.0 0.0 copy-start.2
  128.0 0.0 copy-start.3
  128.0 17.4 %weight_grad.1 = f32[3072,3072]{1,0:T(8,128)} custom-call(bf16[512,3072]{1,0:T(8,128)(2,1)S(1)} %copy-done, bf16[512,3072]{1,0:T(8,128)(2,1)S(1)} %copy-done.1), custom_call_target="tpu_custom_call" | custom-call | flops 9663676416 | bytes 37748736 | tf_op jit(solution)/shard_map/weight_grad/pallas_call | solution.py:328
  145.3 0.0 copy-done.2
  145.3 0.9 copy.8
  146.2 0.0 copy-done.3
  146.2 0.7 copy.9
Async XLA Ops:
  124.2 1.9 %copy-start = (bf16[512,3072]{1,0:T(8,128)(2,1)S(1)}, bf16[512,3072]{1,0:T(8,128)(2,1)}, u32[]{:S(2)}) copy-start(bf16[512,3072]{1,0:T(8,128)(2,1)} %get-tuple-element.9.x_ref) | copy-start | bytes 9437188
  126.1 1.9 %copy-start.1 = (bf16[512,3072]{1,0:T(8,128)(2,1)S(1)}, bf16[512,3072]{1,0:T(8,128)(2,1)}, u32[]{:S(2)}) copy-start(bf16[512,3072]{1,0:T(8,128)(2,1)} %get-tuple-element.10.g_ref) | copy-start | bytes 9437188
  128.0 17.4 %copy-start.2 = (bf16[128,3072]{1,0:T(8,128)(2,1)S(1)}, bf16[128,3072]{1,0:T(8,128)(2,1)}, u32[]{:S(2)}) copy-start(bf16[128,3072]{1,0:T(8,128)(2,1)} %get-tuple-element.14) | copy-start | bytes 2359300
  128.0 18.2 %copy-start.3 = (bf16[64,3072]{1,0:T(8,128)(2,1)S(1)}, bf16[64,3072]{1,0:T(8,128)(2,1)}, u32[]{:S(2)}) copy-start(bf16[64,3072]{1,0:T(8,128)(2,1)} %get-tuple-element.15) | copy-start | bytes 1179652

commit v2 on v1

--- a/solution.py
+++ b/solution.py
@@ -30,7 +30,7 @@
 def chain_kernel(
     n_row, n_col, n_depth, f_tile, d_tile,
     tok_ref, w_hbm, cot_ref,
-    hid_ref, ing_ref, x_ref, g_ref,
+    hid_ref, ing_ref, tail_ref, x_ref, g_ref,
     w_ref, part_ref, relay_a, relay_b, sum_a, sum_b, from_x, from_y,
     back_ref, sib_ref, chip_ref, line_ref,
     w_sem, own_sem,
@@ -62,13 +62,16 @@
 
     sends = []
 
-    def push(src, dst, send_sem, recv_sem, device):
+    def push(src, dst, send_sem, recv_sem, device, when=None):
         copy = pltpu.make_async_remote_copy(
             src_ref=src, dst_ref=dst, send_sem=send_sem, recv_sem=recv_sem,
             device_id=device, device_id_type=MESH,
         )
-        copy.start()
-        sends.append(copy)
+        if when is None:
+            copy.start()
+        else:
+            pl.when(when)(copy.start)
+        sends.append((copy, when))
 
     def arrived(dst, recv_sem):
         pltpu.make_async_remote_copy(
@@ -106,22 +109,37 @@
 
     me = col * n_depth + depth
     own_copies = []
-    for k in range(chunks):
+
+    def start_tokens(k):
         src = tok_ref.at[pl.ds(k * piece, piece), :]
-        for o in range(1, n_col):
-            push(src, x_at(k, me), line_send.at[k, o], x_recv.at[k, me], dev_c[o])
-        for o in range(1, n_depth):
-            push(src, x_at(k, me), sib_send.at[k, o, 0], x_recv.at[k, me], dev_d[o])
+
+        push(src, x_at(k, me), line_send.at[k, 0, 0], x_recv.at[k, me], (row, col + 1, depth), col + 1 < n_col)
+        push(src, x_at(k, me), line_send.at[k, 1, 0], x_recv.at[k, me], (row, col - 1, depth), col > 0)
+        for q in range(1, n_depth):
+            push(src, x_at(k, me), sib_send.at[k, q, 0, 0], x_recv.at[k, me], dev_d[q])
         own = pltpu.make_async_copy(src, x_at(k, me), own_sem.at[k])
         own.start()
         own_copies.append(own)
 
-    def gather_tokens(k):
-        for o in range(1, n_col):
-            block = cols[o] * n_depth + depth
-            arrived(x_at(k, block), x_recv.at[k, block])
+    def pass_tokens(k, s):
+        for way, step in ((0, 1), (1, -1)):
+            origin = col - step * (s + 1)
+            here = jnp.logical_and(origin >= 0, origin < n_col)
+            onward = jnp.logical_and(here, col + 1 < n_col if step == 1 else col > 0)
+
+            block = jnp.clip(origin, 0, n_col - 1) * n_depth + depth
+            spot, sem = x_at(k, block), x_recv.at[k, block]
+
+            @pl.when(here)
+            def _():
+                arrived(spot, sem)
+
+            if s < n_col - 2:
+                push(spot, spot, line_send.at[k, way, s + 1], sem, (row, col + step, depth), onward)
             for q in range(1, n_depth):
-                push(x_at(k, block), x_at(k, block), sib_send.at[k, q, o], x_recv.at[k, block], dev_d[q])
+                push(spot, spot, sib_send.at[k, q, way, s + 1], sem, dev_d[q], here)
+
+    def finish_tokens(k):
         for q in range(1, n_depth):
             for o in range(n_col):
                 block = cols[o] * n_depth + depths[q]
@@ -204,6 +222,9 @@
         for q in range(1, n_depth):
             arrived(sib_ref.at[q - 1, k, :, span], sb_recv.at[k, i, q])
             total = total + sib_ref[q - 1, k, :, span].astype(f32)
+        if k == chunks - 1:
+            tail_ref[:, span] = total.astype(bf16)
+            return
         chip_ref[k, :, span] = total.astype(bf16)
         for o in range(1, n_col):
             push(
@@ -220,17 +241,24 @@
             total = total + line_ref[o - 1, k, :, span].astype(f32)
         ing_ref[pl.ds(k * piece, piece), span] = total.astype(bf16)
 
-    gather_tokens(0)
+    last = chunks - 1
+    start_tokens(0)
+    for s in range(n_col - 1):
+        pass_tokens(0, s)
+    for k in range(1, chunks):
+        start_tokens(k)
+    finish_tokens(0)
     weight_copy.wait()
     for k in range(chunks):
-        if k:
-            gather_tokens(k)
+        passes = list(range(n_col - 1)) if k < last else []
         for j in range(nf):
             up(k, j)
             if j:
                 relay(k, j - 1)
             if k:
                 forward(k - 1, j)
+            if passes and j == nf // 2:
+                pass_tokens(k + 1, passes.pop(0))
         relay(k, nf - 1)
         if k:
             for j in range(nf):
@@ -242,9 +270,17 @@
             chip_sum(k - 1, nd - 1)
         for j in range(nf):
             activate(k, j)
-    last = chunks - 1
+            if passes:
+                pass_tokens(k + 1, passes.pop(0))
+        while passes:
+            pass_tokens(k + 1, passes.pop(0))
+        if k < last:
+            finish_tokens(k + 1)
     for j in range(nf):
         forward(last, j)
+    for k in range(last):
+        for i in range(nd):
+            line_sum(k, i)
     for j in range(nf):
         gathered(last, j)
     for i in range(nd):
@@ -252,11 +288,11 @@
         if i:
             chip_sum(last, i - 1)
     chip_sum(last, nd - 1)
-    for k in range(chunks):
-        for i in range(nd):
-            line_sum(k, i)
-    for copy in sends:
-        copy.wait_send()
+    for copy, when in sends:
+        if when is None:
+            copy.wait_send()
+        else:
+            pl.when(when)(copy.wait_send)
 
 
 def chain(n_row, n_col, n_depth, tokens, weight, cotangent):
@@ -276,12 +312,13 @@
         functools.partial(chain_kernel, n_row, n_col, n_depth, f_tile, d_tile),
         out_shape=[
             jax.ShapeDtypeStruct((own_rows, f_size), bf16),
-            jax.ShapeDtypeStruct((own_tokens, d_size), bf16),
+            jax.ShapeDtypeStruct((own_tokens - piece, d_size), bf16),
+            jax.ShapeDtypeStruct((n_col * piece, d_size), bf16),
             jax.ShapeDtypeStruct((all_tokens, d_size), bf16),
             jax.ShapeDtypeStruct((all_tokens, f_size), bf16),
         ],
         in_specs=[whole, pl.BlockSpec(memory_space=pl.ANY), whole],
-        out_specs=[whole] * 4,
+        out_specs=[whole] * 5,
         scratch_shapes=[
             pltpu.VMEM((d_size, f_size), bf16),
             pltpu.VMEM((all_tokens, f_size), bf16),
@@ -293,10 +330,10 @@
             pltpu.VMEM((own_rows, f_size), bf16),
             pltpu.VMEM((chunks, n_depth, n_col * piece, d_size), bf16),
             pltpu.VMEM((n_depth - 1, chunks, n_col * piece, d_size), bf16),
-            pltpu.VMEM((chunks, n_col * piece, d_size), bf16),
-            pltpu.VMEM((n_col - 1, chunks, piece, d_size), bf16),
+            pltpu.VMEM((chunks - 1, n_col * piece, d_size), bf16),
+            pltpu.VMEM((n_col - 1, chunks - 1, piece, d_size), bf16),
             dma, dma((chunks,)),
-            dma((chunks, n_col)), dma((chunks, n_depth, n_col)), dma((chunks, blocks)),
+            dma((chunks, 2, n_col)), dma((chunks, n_depth, 2, n_col)), dma((chunks, blocks)),
             dma((chunks, nf, 6)), dma((chunks, nf, 6)),
             dma((chunks, nf, 4)), dma((chunks, nf, 4)),
             dma((chunks, nd, n_depth)), dma((chunks, nd, n_depth)),
@@ -312,29 +349,62 @@
     )(tokens, weight, cotangent)
 
 
-def weight_grad_kernel(scale, f_tile, x_ref, g_ref, out_ref):
-    for j in range(g_ref.shape[1] // f_tile):
-        span = pl.ds(j * f_tile, f_tile)
-        out_ref[:, span] = scale * lax.dot_general(
-            x_ref[...], g_ref[:, span], (((0,), (0,)), ((), ())),
-            preferred_element_type=jnp.float32,
+def weight_grad_kernel(scale, f_tile, slots, parts, x_ref, g_ref, out_hbm, held, sems):
+    step, steps = pl.program_id(0), pl.num_programs(0)
+    rows = held.shape[1]
+    size = rows // parts
+    slot = lax.rem(step, slots)
+
+    def piece_of(index, part):
+        at = lax.rem(index, slots)
+        return pltpu.make_async_copy(
+            held.at[at, pl.ds(part * size, size), :],
+            out_hbm.at[pl.ds(pl.multiple_of(index * rows + part * size, size), size), :],
+            sems.at[at, part],
         )
+
+    @pl.when(step >= slots)
+    def _():
+        for part in range(parts):
+            piece_of(step - slots, part).wait()
+
+    flipped = x_ref[...].T
+    for part in range(parts):
+        left = flipped[part * size:(part + 1) * size]
+        for j in range(g_ref.shape[1] // f_tile):
+            span = pl.ds(j * f_tile, f_tile)
+            held[slot, pl.ds(part * size, size), span] = scale * jnp.dot(
+                left, g_ref[:, span], preferred_element_type=jnp.float32
+            )
+        piece_of(step, part).start()
+
+    @pl.when(step == steps - 1)
+    def _():
+        for back in range(slots):
+            for part in range(parts):
+                piece_of(step - back, part).wait()
 
 
 def weight_grad_of(tokens, grads):
     count, d_size = tokens.shape
     f_size = grads.shape[1]
-    d_tile, f_tile = tile_of(d_size, 256), tile_of(f_size, 768)
+    d_tile, f_tile = tile_of(d_size, 512), tile_of(f_size, 768)
+    slots, parts = 3, d_tile // tile_of(d_tile, 256)
+    assert d_size // d_tile >= slots
     return pl.pallas_call(
-        functools.partial(weight_grad_kernel, count ** (-0.5), f_tile),
+        functools.partial(weight_grad_kernel, count ** (-0.5), f_tile, slots, parts),
         grid=(d_size // d_tile,),
         out_shape=jax.ShapeDtypeStruct((d_size, f_size), jnp.float32),
         in_specs=[
             pl.BlockSpec((count, d_tile), lambda i: (0, i)),
             pl.BlockSpec((count, f_size), lambda i: (0, 0)),
         ],
-        out_specs=pl.BlockSpec((d_tile, f_size), lambda i: (i, 0)),
-        compiler_params=pltpu.CompilerParams(vmem_limit_bytes=40 * 2**20),
+        out_specs=pl.BlockSpec(memory_space=pl.ANY),
+        scratch_shapes=[
+            pltpu.VMEM((slots, d_tile, f_size), jnp.float32),
+            pltpu.SemaphoreType.DMA((slots, parts)),
+        ],
+        compiler_params=pltpu.CompilerParams(vmem_limit_bytes=60 * 2**20),
         cost_estimate=pl.CostEstimate(
             flops=2 * count * d_size * f_size, bytes_accessed=4 * d_size * f_size, transcendentals=0
         ),
@@ -346,8 +416,10 @@
     sizes = [mesh.shape[name] for name in ("row", "col", "depth")]
 
     def shards(tokens, weight, cotangent):
-        hidden, input_grad, x_all, g_all = chain(*sizes, tokens, weight, cotangent)
-        return (hidden, input_grad, weight_grad_of(x_all, g_all))
+        hidden, early, tail, x_all, g_all = chain(*sizes, tokens, weight, cotangent)
+        late = lax.psum_scatter(tail, "col", scatter_dimension=0, tiled=True)
+        weight_grad = weight_grad_of(x_all, g_all)
+        return (hidden, jnp.concatenate([early, late], axis=0), weight_grad)
 
     in_specs = (P(("col", "depth"), "row"), P("row", ("col", "depth")), P("row", ("col", "depth")))
     out_specs = (P("row", ("col", "depth")), P(("col", "depth"), "row"), P("row", ("col", "depth")))

time: 147 us -> 143 us (0.973)
  Pallas kernels: 141 us -> 120 us
  between operations: 0.65 us -> 14.1 us
  waiting for transfers between devices: 0 us -> 6.67 us
  local copies, waits for them, and re-layouts: 5.4 us -> 0.89 us
  other arithmetic: 0 us -> 1.7 us
    pallas_call x1, Pallas kernels: 124 us -> 104 us  [chain(): pl.pallas_call(functools.partial(chain_kernel, n_row, n_col, n_depth, f_t...]
    reduce_scatter x0 -> x1, waiting for transfers between devices: none -> 6.65 us  [shards(): late = lax.psum_scatter(tail, 'col', scatter_dimension=0, tiled=True)]
    unnamed x10 -> x5, local copies, waits for them, and re-layouts: 5.4 us -> 0.89 us
    concatenate x0 -> x1, other arithmetic: none -> 1.7 us  [shards(): return (hidden, jnp.concatenate([early, late], axis=0), weight_grad)]
    pallas_call x1, Pallas kernels: 17.4 us -> 15.8 us  [weight_grad_of(): pl.pallas_call(functools.partial(weight_grad_kernel, count ** (-0.5), f_t...]
  transfers between devices with their start and end apart: 0 -> 1, of which waited for: 0 -> 1; matrix products, arithmetic and copies ran while one was open for 0% -> 0% of each run, Pallas kernels for 0% -> 11%
where the time goes in v2:
time: 143 us
  Pallas kernels  120 us (84%)
  between operations  14.1 us (10%)
  waiting for transfers between devices  6.67 us (5%)
  other arithmetic  1.7 us (1%)
    pallas_call x1, Pallas kernels, chain(): pl.pallas_call(functools.partial(chain_kernel, n_row, n_col, n_depth, f_t...  104 us
    pallas_call x1, Pallas kernels, weight_grad_of(): pl.pallas_call(functools.partial(weight_grad_kernel, count ** (-0.5), f_t...  15.8 us
    reduce_scatter x1, waiting for transfers between devices, shards(): late = lax.psum_scatter(tail, 'col', scatter_dimension=0, tiled=True)  6.65 us
  transfers between devices with their start and end apart: 1, of which 1 were waited for; matrix products, arithmetic and copies ran while one was open for 0% of the time, Pallas kernels for 11%

profile of v2, /device:TPU:0, one launch (start us, length us, event | category | flops | bytes accessed | tf_op | source)
XLA Modules:
  0.0 143.2 jit_solution(8906996876449155444)
XLA Ops:
  7.2 0.0 reduce-scatter.2.cloned.1.call-start
  7.2 104.1 %chain.1 = (bf16[128,3072]{1,0:T(8,128)(2,1)}, bf16[32,3072]{1,0:T(8,128)(2,1)}, bf16[128,3072]{1,0:T(8,128)(2,1)}, bf16[512,3072]{1,0:T(8,128)(2,1)}, bf16[512,3072]{1,0:T(8,128)(2,1)}) custom-call(bf16[64,3072]{1,0:T(8,128)(2,1)} %tok_ref.1, bf16[3072,3072]{1,0:T(8,128)(2,1)} %w_hbm.1, bf16[128,3072]{1,0:T(8,128)(2,1)} %cot_ref.1), custom_call_target="tpu_custom_call" | custom-call | flops 19327352832 | bytes 18874368 | tf_op jit(solution)/shard_map/chain/pallas_call | solution.py:311
  111.3 0.0 reduce-scatter.2.cloned.1.call-update
  111.3 0.0 copy-start.1
  111.3 0.0 copy-start
  111.3 15.8 %weight_grad.1 = f32[3072,3072]{1,0:T(8,128)} custom-call(bf16[512,3072]{1,0:T(8,128)(2,1)} %get-tuple-element.11.x_ref, bf16[512,3072]{1,0:T(8,128)(2,1)} %get-tuple-element.12.g_ref), custom_call_target="tpu_custom_call" | custom-call | flops 9663676416 | bytes 37748736 | tf_op jit(solution)/shard_map/weight_grad/pallas_call | solution.py:394
  127.1 6.7 %reduce-scatter.2.cloned.1.call-done = bf16[32,3072]{1,0:T(8,128)(2,1)} async-done(((bf16[128,3072]{1,0:T(8,128)(2,1)}), bf16[32,3072]{1,0:T(8,128)(2,1)}) %reduce-scatter.2.cloned.1.call-update) | async-done | bytes 196624 | tf_op jit(solution)/shard_map/reduce_scatter | solution.py:420
  133.7 0.0 copy-done.1
  133.8 1.7 %pad_maximum_fusion = bf16[64,3072]{1,0:T(8,128)(2,1)} fusion(bf16[32,3072]{1,0:T(8,128)(2,1)} %reduce-scatter.2.cloned.1.call-done, bf16[32,3072]{1,0:T(8,128)(2,1)S(1)} %copy-done.1), kind=kLoop, calls=%fused_computation | loop fusion | flops 786432 | bytes 786432 | tf_op jit(solution)/shard_map/concatenate | solution.py:422
  135.5 0.0 copy-done
  135.5 0.9 copy.7
Async XLA Ops:
  7.2 126.6 %reduce-scatter.2.cloned.1.call-start = ((), (), s32[]{:S(2)}) async-start(), calls=%async_computation.1 | async-start | bytes 983040 | tf_op jit(solution)/shard_map/reduce_scatter | solution.py:420
  111.3 22.4 %copy-start.1 = (bf16[32,3072]{1,0:T(8,128)(2,1)S(1)}, bf16[32,3072]{1,0:T(8,128)(2,1)}, u32[]{:S(2)}) copy-start(bf16[32,3072]{1,0:T(8,128)(2,1)} %get-tuple-element.9) | copy-start | bytes 589828
  111.3 24.1 %copy-start = (bf16[128,3072]{1,0:T(8,128)(2,1)S(1)}, bf16[128,3072]{1,0:T(8,128)(2,1)}, u32[]{:S(2)}) copy-start(bf16[128,3072]{1,0:T(8,128)(2,1)} %get-tuple-element.16) | copy-start | bytes 2359300
Sparse Core Ops, SparseCore 0:
  111.4 22.2 reduce-scatter.1
